TPU v7x, 32 devices: a whole 2x2x4 slice. The times are simulated.
32 devices in a mesh: lat: 16 (over z, y, core), lon: 2 (over x).
Axes of the slice: x: 2, y: 2, z: 4, core: 2. Of those that a mesh axis runs over, the one named last changes fastest.
Arguments:
- source_field: bfloat16 [384, 768, 384], P('lat', 'lon'), may hold values from -6 to 6
- cotangent: bfloat16 [384, 768, 384], P('lat', 'lon'), may hold values from -6 to 6
- weight: bfloat16 [3, 384, 384], replicated, may hold values from -0.1875 to 0.1875
- spectral_gain: float32 [384, 384], replicated, may hold values from 0.1 to 1.9
- legendre: bfloat16 [384, 384, 384], P(('lat', 'lon')), may hold values from -0.3125 to 0.3125
- support_lat: int32 [384, 16], replicated, may hold values from -2 to 2
- support_lon: int32 [384, 16], replicated, may hold values from -4 to 4
- support_val: float32 [384, 16, 3], replicated, may hold values from -1.5 to 1.5
- order_map: int32 [384], replicated, may hold values from 0 to 383, each once
Outputs:
- result: bfloat16 [384, 768, 384], P('lat', 'lon')
- grad_input: bfloat16 [384, 768, 384], P('lat', 'lon')
- grad_weight: float32 [3, 384, 384], replicated
- grad_gain: float32 [384, 384], replicated
Inputs may be any that keep to these rules, and one draw needn't show every extreme that they name: `order_map`: each order appears once.
All inputs are finite; a program needn't handle non-finite values.
Results may differ from a plain program's by a relative error of at most 0.009.
Values may be sent and summed in bfloat16 or wider, within the bound.
A program may use at most 512 MiB of HBM per device.

v0:
```python
import math

import jax
import jax.numpy as jnp
from jax import lax
from jax.sharding import PartitionSpec as P

NLON = 768
M = 384
K = 3
H = 2
DW = 4


SQRT_HALF = 0.7071067811865476
INV_SQRT_TAU = 0.3989422804014327


def extended(block, sides, width, periodic):
    for axis, dim in sides:
        count = lax.axis_size(axis)
        forward = [(i, i + 1) for i in range(count - 1)]
        if periodic:
            forward.append((count - 1, 0))
        backward = [(target, source) for source, target in forward]
        low = lax.ppermute(
            lax.slice_in_dim(block, block.shape[dim] - width, None, axis=dim), axis, forward
        )
        high = lax.ppermute(lax.slice_in_dim(block, 0, width, axis=dim), axis, backward)
        block = jnp.concatenate([low, block, high], axis=dim)
    return block


def gelu_value(values):
    return 0.5 * values * (1.0 + lax.erf(values * SQRT_HALF))


def gelu_slope(values):
    return 0.5 * (1.0 + lax.erf(values * SQRT_HALF)) + values * INV_SQRT_TAU * jnp.exp(
        -0.5 * values * values
    )


def tap_table(support_lat, support_lon, support_val):
    lat_steps = jnp.arange(2 * H + 1, dtype=jnp.int32) - H
    lon_steps = jnp.arange(2 * DW + 1, dtype=jnp.int32) - DW
    lat_onehot = (support_lat[:, :, None] == lat_steps[None, None, :]).astype(jnp.float32)
    lon_onehot = (support_lon[:, :, None] == lon_steps[None, None, :]).astype(jnp.float32)
    return jnp.einsum(
        "tsk,tsa,tsd->tkad", support_val, lat_onehot, lon_onehot, precision=lax.Precision.HIGHEST
    )


def dft_table(order_map):
    frequency = jnp.repeat(order_map, 2)
    component = jnp.arange(frequency.shape[0], dtype=jnp.int32) % 2
    longitude = jnp.arange(NLON, dtype=jnp.int32)
    cycles = longitude[:, None] * frequency[None, :] % NLON
    angles = cycles.astype(jnp.float32) * (2.0 * math.pi / NLON)
    matrix = jnp.where(component[None, :] == 0, jnp.cos(angles), -jnp.sin(angles)) * math.sqrt(
        2.0 / NLON
    )
    return matrix.astype(jnp.bfloat16)


def apply_taps(padded, tap_rows, row_count, col_count, mirror):
    wide_count = col_count + 2 * DW
    out_cols = jnp.arange(col_count, dtype=jnp.int32)
    in_cols = jnp.arange(wide_count, dtype=jnp.int32)
    offsets = jnp.arange(2 * DW + 1, dtype=jnp.int32)
    distance = in_cols[None, :] - out_cols[:, None]
    if mirror:
        distance = 2 * DW - distance
    band_onehot = (distance[:, :, None] == offsets[None, None, :]).astype(jnp.float32)
    coef_list = []
    window_list = []
    for lat_tap in range(2 * H + 1):
        if mirror:
            row_start = 2 * H - lat_tap
            coef_list.append(tap_rows[row_start : row_start + row_count, :, lat_tap, :])
        else:
            row_start = lat_tap
            coef_list.append(tap_rows[H : H + row_count, :, lat_tap, :])
        window_list.append(padded[row_start : row_start + row_count])
    coef_stack = jnp.stack(coef_list, axis=2)
    window_stack = jnp.stack(window_list, axis=1).astype(jnp.float32)
    band_matrix = jnp.einsum(
        "tkad,pqd->tpkaq", coef_stack, band_onehot, precision=lax.Precision.HIGHEST
    )
    summed = jnp.einsum(
        "tpkaq,taqc->tpkc", band_matrix, window_stack, precision=lax.Precision.HIGHEST
    )
    return summed.astype(jnp.bfloat16)


def padded_field(field):
    lon_padded = extended(field, (("lon", 1),), DW, True)
    return extended(lon_padded, (("lat", 0),), H, False)


def to_lines(field):
    moved = lax.all_to_all(field, "lon", split_axis=2, concat_axis=1, tiled=True)
    return moved


def to_grid(field):
    moved = lax.all_to_all(field, "lon", split_axis=1, concat_axis=2, tiled=True)
    return moved


def to_spec(field):
    moved = lax.all_to_all(field, "lat", split_axis=1, concat_axis=0, tiled=True)
    return moved


def to_line_rows(field):
    moved = lax.all_to_all(field, "lat", split_axis=0, concat_axis=1, tiled=True)
    return moved


def legendre_in(spectral, table_rows):
    lat_total, col_total, chan_total = spectral.shape
    halves = spectral.reshape(lat_total, col_total // 2, 2, chan_total)
    return jnp.einsum("olt,toqc->olqc", table_rows, halves, preferred_element_type=jnp.float32)


def legendre_out(coefficients, table_rows):
    synthesis = jnp.einsum(
        "olt,olqc->toqc", table_rows, coefficients, preferred_element_type=jnp.float32
    )
    lat_total, order_count, two_parts, chan_total = synthesis.shape
    return synthesis.reshape(lat_total, order_count * two_parts, chan_total)


def body(
    source_field,
    cotangent,
    weight,
    spectral_gain,
    legendre,
    support_lat,
    support_lon,
    support_val,
    order_map,
):
    row_count, col_count, chan_count = source_field.shape
    lon_devices = lax.axis_size("lon")
    lat_total = row_count * lax.axis_size("lat")
    band_index = lax.axis_index("lat")
    block_index = lax.axis_index("lon")
    tap_weights = tap_table(support_lat, support_lon, support_val)
    tap_pad = jnp.pad(tap_weights, ((H, H), (0, 0), (0, 0), (0, 0)))
    tap_rows = lax.dynamic_slice_in_dim(tap_pad, band_index * row_count, row_count + 2 * H, 0)
    dft_matrix = dft_table(order_map)
    flat_weight = weight.reshape(K * chan_count, chan_count)
    all_rows = jnp.arange(lat_total, dtype=jnp.int32).astype(jnp.float32)
    quad_all = jnp.sin(math.pi * (all_rows + 0.5) / lat_total)
    line_quad = lax.dynamic_slice_in_dim(quad_all, band_index * row_count, row_count, 0)
    table_rows = lax.all_gather(legendre, "lon", axis=0, tiled=True)
    chan_share = chan_count // lon_devices
    gain_rows = lax.dynamic_slice_in_dim(spectral_gain, block_index * chan_share, chan_share, 1)
    source_pad = padded_field(source_field)
    taps_flat = apply_taps(source_pad, tap_rows, row_count, col_count, False).reshape(
        row_count * col_count, K * chan_count
    )
    conv_out = jnp.dot(taps_flat, flat_weight, preferred_element_type=jnp.float32).astype(
        jnp.bfloat16
    )
    conv_wide = conv_out.astype(jnp.float32).reshape(row_count, col_count, chan_count)
    hidden = gelu_value(conv_wide).astype(jnp.bfloat16)
    line_field = to_lines(hidden)
    line_spec = jnp.einsum(
        "tpc,pj->tjc", line_field, dft_matrix, preferred_element_type=jnp.float32
    )
    spectral = to_spec((line_spec * line_quad[:, None, None]).astype(jnp.bfloat16))
    coefficients = legendre_in(spectral, table_rows)
    filtered = (gain_rows[None, :, None, :] * coefficients).astype(jnp.bfloat16)
    synthesized = legendre_out(filtered, table_rows).astype(jnp.bfloat16)
    synth_lines = to_line_rows(synthesized)
    branch = jnp.einsum(
        "tjc,pj->tpc", synth_lines, dft_matrix, preferred_element_type=jnp.float32
    ).astype(jnp.bfloat16)
    branch_grid = to_grid(branch)
    result = (conv_wide + branch_grid.astype(jnp.float32)).astype(jnp.bfloat16)
    cot_lines = to_lines(cotangent)
    cot_line_spec = jnp.einsum(
        "tpc,pj->tjc", cot_lines, dft_matrix, preferred_element_type=jnp.float32
    )
    cot_spectral = to_spec(cot_line_spec.astype(jnp.bfloat16))
    cot_coefficients = legendre_in(cot_spectral, table_rows)
    gain_part = jnp.sum(coefficients * cot_coefficients, axis=(0, 2))
    cot_filtered = (gain_rows[None, :, None, :] * cot_coefficients).astype(jnp.bfloat16)
    cot_synth = legendre_out(cot_filtered, table_rows)
    cot_synth = (cot_synth * quad_all[:, None, None]).astype(jnp.bfloat16)
    cot_synth_lines = to_line_rows(cot_synth)
    cot_hidden = jnp.einsum(
        "tjc,pj->tpc", cot_synth_lines, dft_matrix, preferred_element_type=jnp.float32
    ).astype(jnp.bfloat16)
    cot_hidden_grid = to_grid(cot_hidden)
    cot_conv = (
        cotangent.astype(jnp.float32) + cot_hidden_grid.astype(jnp.float32) * gelu_slope(conv_wide)
    ).astype(jnp.bfloat16)
    cot_flat = cot_conv.reshape(row_count * col_count, chan_count)
    weight_part = lax.dot_general(
        taps_flat, cot_flat, (((0,), (0,)), ((), ())), preferred_element_type=jnp.float32
    )
    cot_pad = padded_field(cot_conv)
    back_taps = apply_taps(cot_pad, tap_rows, row_count, col_count, True).reshape(
        row_count * col_count, K, chan_count
    )
    grad_input = jnp.einsum("nkf,kcf->nc", back_taps, weight, preferred_element_type=jnp.float32)
    grad_input = grad_input.astype(jnp.bfloat16).reshape(row_count, col_count, chan_count)
    weight_total = lax.psum(weight_part, ("lat", "lon"))
    gain_band = lax.psum(gain_part, "lat")
    gain_total = lax.all_gather(gain_band, "lon", axis=1, tiled=True)
    grad_weight = (weight_total / math.sqrt(1.0 * lat_total * NLON)).reshape(
        K, chan_count, chan_count
    )
    grad_gain = gain_total / math.sqrt(2.0 * M)
    return (result, grad_input, grad_weight, grad_gain)


def solution(mesh):
    return jax.shard_map(
        body,
        mesh=mesh,
        in_specs=(
            P("lat", "lon", None),
            P("lat", "lon", None),
            P(),
            P(),
            P(("lat", "lon"), None, None),
            P(),
            P(),
            P(),
            P(),
        ),
        out_specs=(P("lat", "lon", None), P("lat", "lon", None), P(), P()),
        check_vma=False,
    )
```

profile of v0, /device:TPU:9, one launch (start us, length us, event | category | flops | bytes accessed | tf_op | source)
XLA Modules:
  0.0 2644.8 jit_solution(2912566899447401050)
XLA Ops:
  46.3 121.5 %convolution_bitcast_fusion.1 = f32[24,384,3,5,392]{4,0,3,2,1:T(8,128)} fusion(s32[384,392]{1,0:T(8,128)S(1)} %iota_subtract_fusion, f32[24,3,5,9]{0,3,2,1:T(8,128)S(1)} %copy.264), kind=kOutput, calls=%fused_computation.5 | convolution fusion | flops 5853883392 | bytes 217375392 | tf_op jit(solution)/shard_map/tkad,pqd->tpkaq/dot_general | solution.py:87
  168.6 24.9 pad_maximum_fusion
  222.0 415.7 %bitcast_convert_fusion.1 = bf16[24,384,3,384]{3,1,2,0:T(8,128)(2,1)} fusion(bf16[24,5,392,384]{3,2,1,0:T(8,128)(2,1)} %fusion.37, f32[24,384,3,5,392]{4,0,3,2,1:T(8,128)} %convolution_bitcast_fusion.1), kind=kOutput, calls=%fused_computation.7 | convolution fusion | flops 249718505472 | bytes 274120704 | tf_op jit(solution)/shard_map/tpkaq,taqc->tpkc/dot_general | solution.py:90
  637.7 27.6 %copy.270 = bf16[24,384,3,384]{1,0,3,2:T(8,128)(2,1)} copy(bf16[24,384,3,384]{3,1,2,0:T(8,128)(2,1)} %bitcast_convert_fusion.1) | data formatting | bytes 42467328 | tf_op jit(solution)/shard_map/convert_element_type | solution.py:93
  665.3 15.5 copy.322
  680.8 16.3 convolution_convert_fusion
  734.1 16.1 all_to_all.103
  750.3 19.8 fusion.82
  779.0 13.4 copy.290
  819.4 16.1 all_to_all.91
  835.6 19.7 fusion.80
  864.9 13.4 copy.275
  878.3 131.9 %all-to-all-done.5 = bf16[24,768,192]{2,0,1:T(8,128)(2,1)} async-done(((bf16[24,768,192]{2,0,1:T(8,128)(2,1)}), bf16[24,768,192]{2,0,1:T(8,128)(2,1)}, u32[]{:S(2)}, u32[]{:S(2)}) %all-to-all-start.5) | async-done | bytes 7077920 | tf_op jit(solution)/shard_map/all_to_all | solution.py:112
  1027.2 192.7 %all-to-all-done.1 = bf16[24,768,192]{2,0,1:T(8,128)(2,1)} async-done(((bf16[24,768,192]{2,0,1:T(8,128)(2,1)}), bf16[24,768,192]{2,0,1:T(8,128)(2,1)}, u32[]{:S(2)}, u32[]{:S(2)}) %all-to-all-start.1) | async-done | bytes 7077920 | tf_op jit(solution)/shard_map/all_to_all | solution.py:112
  1241.6 17.2 fusion.19
  1326.7 177.6 %all-to-all-done.6 = bf16[384,48,192]{2,1,0:T(8,128)(2,1)} async-done(((bf16[384,48,192]{2,1,0:T(8,128)(2,1)}), bf16[384,48,192]{2,1,0:T(8,128)(2,1)}, u32[]{:S(2)}, u32[]{:S(2)}) %all-to-all-start.6) | async-done | bytes 7077920 | tf_op jit(solution)/shard_map/all_to_all | solution.py:117
  1531.2 19.9 fusion.79
  1560.0 13.4 copy.297
  1573.3 140.7 %all-to-all-done.2 = bf16[384,48,192]{2,1,0:T(8,128)(2,1)} async-done(((bf16[384,48,192]{2,1,0:T(8,128)(2,1)}), bf16[384,48,192]{2,1,0:T(8,128)(2,1)}, u32[]{:S(2)}, u32[]{:S(2)}) %all-to-all-start.2) | async-done | bytes 7077920 | tf_op jit(solution)/shard_map/all_to_all | solution.py:117
  1744.2 19.9 fusion.81
  1786.5 37.8 %all-to-all-done.7 = bf16[24,768,192]{2,0,1:T(8,128)(2,1)} async-done(((bf16[24,768,192]{2,0,1:T(8,128)(2,1)}), bf16[24,768,192]{2,0,1:T(8,128)(2,1)}, u32[]{:S(2)}, u32[]{:S(2)}) %all-to-all-start.7) | async-done | bytes 7077920 | tf_op jit(solution)/shard_map/all_to_all | solution.py:107
  1831.7 121.5 %convolution_bitcast_fusion = f32[24,384,3,5,392]{4,0,3,2,1:T(8,128)} fusion(s32[384,392]{1,0:T(8,128)S(1)} %broadcast_subtract_fusion, f32[24,3,5,9]{0,3,2,1:T(8,128)S(1)} %copy.286), kind=kOutput, calls=%fused_computation.4 | convolution fusion | flops 5853883392 | bytes 217375392 | tf_op jit(solution)/shard_map/tkad,pqd->tpkaq/dot_general | solution.py:87
  1973.3 15.5 reshape.122
  2001.0 15.1 copy.300
  2028.4 15.4 reshape.121
  2056.0 15.1 copy.285
  2071.2 17.9 fusion.15
  2113.8 18.0 fusion.109
  2132.7 24.9 maximum_maximum_fusion.1
  2186.6 415.4 %bitcast_convert_fusion = bf16[24,384,3,384]{3,1,2,0:T(8,128)(2,1)} fusion(bf16[24,5,392,384]{3,2,1,0:T(8,128)(2,1)} %fusion.33, f32[24,384,3,5,392]{4,0,3,2,1:T(8,128)} %convolution_bitcast_fusion), kind=kOutput, calls=%fused_computation.6 | convolution fusion | flops 249718505472 | bytes 274120704 | tf_op jit(solution)/shard_map/tpkaq,taqc->tpkc/dot_general | solution.py:90
  2602.0 15.2 copy.306
  2617.2 18.0 bitcast_convert_fusion.2
  (149 shorter events, 467.2 us)
Async XLA Ops:
  7.2 673.6 %copy-start = (bf16[3,384,384]{2,1,0:T(8,128)(2,1)S(1)}, bf16[3,384,384]{2,1,0:T(8,128)(2,1)}, u32[]{:S(2)}) copy-start(bf16[3,384,384]{2,1,0:T(8,128)(2,1)} %param.11) | copy-start | bytes 2654212
  8.3 25.7 collective-permute-start
  9.6 24.4 collective-permute-start.1
  20.1 6.8 copy-start.10
  20.1 6.9 copy-start.9
  20.1 7.2 copy-start.11
  20.1 695.2 %all-to-all-start.4 = ((bf16[24,384,384]{1,0,2:T(8,128)(2,1)}), bf16[24,384,384]{1,0,2:T(8,128)(2,1)}, u32[]{:S(2)}, u32[]{:S(2)}) async-start(bf16[24,384,384]{1,0,2:T(8,128)(2,1)} %copy.287), calls=%async_computation.4 | async-start | bytes 14155776 | tf_op jit(solution)/shard_map/all_to_all | solution.py:102
  39.9 127.9 %collective-permute-start.2 = (bf16[2,392,384]{2,1,0:T(8,128)(2,1)}, bf16[2,392,384]{2,1,0:T(8,128)(2,1)S(1)}, u32[]{:S(2)}, u32[]{:S(2)}) collective-permute-start(bf16[2,392,384]{2,1,0:T(8,128)(2,1)} %get-tuple-element.31), channel_id=1, source_target_pairs={{0,2},{2,4},{4,6},{6,8},{8,10},{10,12},{12,14},{14,16},{16,18},{18... | collective-permute-start | bytes 1806344 | tf_op jit(solution)/shard_map/ppermute | solution.py:26
  44.1 124.4 %collective-permute-start.3 = (bf16[2,392,384]{2,1,0:T(8,128)(2,1)S(1)}, bf16[2,392,384]{2,1,0:T(8,128)(2,1)}, u32[]{:S(2)}, u32[]{:S(2)}) collective-permute-start(bf16[2,392,384]{2,1,0:T(8,128)(2,1)S(1)} %get-tuple-element.30), channel_id=1, source_target_pairs={{2,0},{4,2},{6,4},{8,6},{10,8},{12,10},{14,12},{16,14},{18,16},{20... | collective-permute-start | bytes 1806344 | tf_op jit(solution)/shard_map/ppermute | solution.py:29
  196.5 10.7 slice-start.2
  200.3 6.9 slice-start.3
  211.5 6.9 slice-start.6
  211.5 6.9 slice-start.7
  715.3 83.9 %all-to-all-start = ((bf16[24,384,384]{1,0,2:T(8,128)(2,1)}), bf16[24,384,384]{1,0,2:T(8,128)(2,1)}, u32[]{:S(2)}, u32[]{:S(2)}) async-start(bf16[24,384,384]{1,0,2:T(8,128)(2,1)} %copy.272), calls=%async_computation | async-start | bytes 14155776 | tf_op jit(solution)/shard_map/all_to_all | solution.py:102
  799.2 211.0 %all-to-all-start.5 = ((bf16[24,768,192]{2,0,1:T(8,128)(2,1)}), bf16[24,768,192]{2,0,1:T(8,128)(2,1)}, u32[]{:S(2)}, u32[]{:S(2)}) async-start(bf16[24,768,192]{2,0,1:T(8,128)(2,1)} %copy.290), calls=%async_computation.5 | async-start | bytes 18874368 | tf_op jit(solution)/shard_map/all_to_all | solution.py:112
  878.3 139.7 %copy-start.8 = (f32[384,384]{1,0:T(8,128)S(1)}, f32[384,384]{1,0:T(8,128)}, u32[]{:S(2)}) copy-start(f32[384,384]{1,0:T(8,128)} %param.12) | copy-start | bytes 1769476
  1010.2 209.7 %all-to-all-start.1 = ((bf16[24,768,192]{2,0,1:T(8,128)(2,1)}), bf16[24,768,192]{2,0,1:T(8,128)(2,1)}, u32[]{:S(2)}, u32[]{:S(2)}) async-start(bf16[24,768,192]{2,0,1:T(8,128)(2,1)} %copy.275), calls=%async_computation.1 | async-start | bytes 18874368 | tf_op jit(solution)/shard_map/all_to_all | solution.py:112
  1017.2 211.2 %all-gather.2.cloned.1.call-start = ((), (), s32[]{:S(2)}) async-start(), calls=%async_computation.8 | async-start | bytes 10616832 | tf_op jit(solution)/shard_map/all_gather | solution.py:159
  1294.4 209.9 %all-to-all-start.6 = ((bf16[384,48,192]{2,1,0:T(8,128)(2,1)}), bf16[384,48,192]{2,1,0:T(8,128)(2,1)}, u32[]{:S(2)}, u32[]{:S(2)}) async-start(bf16[384,48,192]{2,1,0:T(8,128)(2,1)} %copy.294), calls=%async_computation.6 | async-start | bytes 18874368 | tf_op jit(solution)/shard_map/all_to_all | solution.py:117
  1504.3 209.7 %all-to-all-start.2 = ((bf16[384,48,192]{2,1,0:T(8,128)(2,1)}), bf16[384,48,192]{2,1,0:T(8,128)(2,1)}, u32[]{:S(2)}, u32[]{:S(2)}) async-start(bf16[384,48,192]{2,1,0:T(8,128)(2,1)} %copy.279), calls=%async_computation.2 | async-start | bytes 18874368 | tf_op jit(solution)/shard_map/all_to_all | solution.py:117
  1714.1 110.2 %all-to-all-start.7 = ((bf16[24,768,192]{2,0,1:T(8,128)(2,1)}), bf16[24,768,192]{2,0,1:T(8,128)(2,1)}, u32[]{:S(2)}, u32[]{:S(2)}) async-start(bf16[24,768,192]{2,0,1:T(8,128)(2,1)} %copy.297), calls=%async_computation.7 | async-start | bytes 18874368 | tf_op jit(solution)/shard_map/all_to_all | solution.py:107
  1721.5 231.8 %all-reduce.6.cloned.1.call-start = ((), (), s32[]{:S(2)}) async-start(), calls=%async_computation.10 | async-start | bytes 589824 | tf_op jit(solution)/shard_map/psum | solution.py:214
  1824.2 191.9 %all-to-all-start.3 = ((bf16[24,768,192]{2,0,1:T(8,128)(2,1)}), bf16[24,768,192]{2,0,1:T(8,128)(2,1)}, u32[]{:S(2)}, u32[]{:S(2)}) async-start(bf16[24,768,192]{2,0,1:T(8,128)(2,1)} %copy.282), calls=%async_computation.3 | async-start | bytes 18874368 | tf_op jit(solution)/shard_map/all_to_all | solution.py:107
  1831.7 803.6 %all-reduce.4.cloned.1.call-start = ((), (), s32[]{:S(2)}) async-start(), calls=%async_computation.9 | async-start | bytes 3538944 | tf_op jit(solution)/shard_map/psum | solution.py:213
  2092.1 3.3 collective-permute-start.4
  2093.3 3.2 collective-permute-start.5
  2101.5 30.3 %collective-permute-start.6 = (bf16[2,392,384]{2,1,0:T(8,128)(2,1)S(1)}, bf16[2,392,384]{2,1,0:T(8,128)(2,1)S(1)}, u32[]{:S(2)}, u32[]{:S(2)}) collective-permute-start(bf16[2,392,384]{2,1,0:T(8,128)(2,1)S(1)} %get-tuple-element.27), channel_id=1, source_target_pairs={{2,0},{4,2},{6,4},{8,6},{10,8},{12,10},{14,12},{16,14},{18,16},{20... | collective-permute-start | bytes 1806344 | tf_op jit(solution)/shard_map/ppermute | solution.py:29
  2107.8 24.8 collective-permute-start.7
  2160.7 10.8 slice-start
  2164.5 7.0 slice-start.1
  2176.0 6.9 slice-start.4
  2176.0 6.9 slice-start.5
  (8 other events, 22.5 us)
Sparse Core Ops, SparseCore 0:
  1019.6 88.8 all-gather.1
  1726.3 90.6 all-reduce.5
  2131.9 129.1 all-reduce.3
where the time goes:
time: 2660 us; the launch traced here: 2640 us
  matrix products  1260 us (47%)
  waiting for transfers between devices  690 us (26%)
  local copies, waits for them, and re-layouts  448 us (17%)
  other arithmetic  141 us (5%)
  starting transfers between devices  80 us (3%)
    dot_general x2, matrix products, apply_taps(): jnp.einsum('tpkaq,taqc->tpkc', band_matrix, window_stack, precision=lax.P...  831 us
    all_to_all x2, waiting for transfers between devices, to_spec(): lax.all_to_all(field, 'lat', split_axis=1, concat_axis=0, tiled=True)  325 us
    all_to_all x2, waiting for transfers between devices, to_line_rows(): lax.all_to_all(field, 'lat', split_axis=0, concat_axis=1, tiled=True)  318 us
    dot_general x2, matrix products, apply_taps(): jnp.einsum('tkad,pqd->tpkaq', coef_stack, band_onehot, precision=lax.Prec...  243 us
    unnamed x4, matrix products  79.3 us
    unnamed x54, local copies, waits for them, and re-layouts  78.4 us
    concatenate x4, other arithmetic, extended(): block = jnp.concatenate([low, block, high], axis=dim)  59.7 us
    all_to_all x4, local copies, waits for them, and re-layouts, to_lines(): lax.all_to_all(field, 'lon', split_axis=2, concat_axis=1, tiled=True)  55.7 us
  transfers between devices with their start and end apart: 19, of which 8 were waited for; matrix products, arithmetic and copies ran while one was open for 63% of the time, Pallas kernels for 0%

commit v1 on v0

v1 whole, which is shorter than its diff:
```python
import math

import jax
import jax.numpy as jnp
from jax import lax
from jax.experimental import pallas as pl
from jax.experimental.pallas import tpu as pltpu
from jax.sharding import PartitionSpec as P

NLON = 768
M = 384
K = 3
H = 2
DW = 4


SQRT_HALF = 0.7071067811865476
INV_SQRT_TAU = 0.3989422804014327


def extended(block, sides, width, periodic):
    for axis, dim in sides:
        count = lax.axis_size(axis)
        forward = [(i, i + 1) for i in range(count - 1)]
        if periodic:
            forward.append((count - 1, 0))
        backward = [(target, source) for source, target in forward]
        low = lax.ppermute(
            lax.slice_in_dim(block, block.shape[dim] - width, None, axis=dim), axis, forward
        )
        high = lax.ppermute(lax.slice_in_dim(block, 0, width, axis=dim), axis, backward)
        block = jnp.concatenate([low, block, high], axis=dim)
    return block


def gelu_value(values):
    return 0.5 * values * (1.0 + lax.erf(values * SQRT_HALF))


def gelu_slope(values):
    return 0.5 * (1.0 + lax.erf(values * SQRT_HALF)) + values * INV_SQRT_TAU * jnp.exp(
        -0.5 * values * values
    )


def tap_table(support_lat, support_lon, support_val):
    lat_steps = jnp.arange(2 * H + 1, dtype=jnp.int32) - H
    lon_steps = jnp.arange(2 * DW + 1, dtype=jnp.int32) - DW
    lat_onehot = (support_lat[:, :, None] == lat_steps[None, None, :]).astype(jnp.float32)
    lon_onehot = (support_lon[:, :, None] == lon_steps[None, None, :]).astype(jnp.float32)
    return jnp.einsum(
        "tsk,tsa,tsd->tkad", support_val, lat_onehot, lon_onehot, precision=lax.Precision.HIGHEST
    )


def dft_table(order_map):
    frequency = jnp.repeat(order_map, 2)
    component = jnp.arange(frequency.shape[0], dtype=jnp.int32) % 2
    longitude = jnp.arange(NLON, dtype=jnp.int32)
    cycles = longitude[:, None] * frequency[None, :] % NLON
    angles = cycles.astype(jnp.float32) * (2.0 * math.pi / NLON)
    matrix = jnp.where(component[None, :] == 0, jnp.cos(angles), -jnp.sin(angles)) * math.sqrt(
        2.0 / NLON
    )
    return matrix.astype(jnp.bfloat16)


P_BLOCK = 96
Q_BLOCK = 128
N_LAT_TAPS = 2 * H + 1


def tap_coefficients(tap_rows, row_count, mirror):
    coef_list = []
    for place in range(N_LAT_TAPS):
        if mirror:
            taken = tap_rows[place : place + row_count, :, N_LAT_TAPS - 1 - place, ::-1]
        else:
            taken = tap_rows[H : H + row_count, :, place, :]
        coef_list.append(taken)
    coefs = jnp.stack(coef_list, axis=2).reshape(row_count, K * N_LAT_TAPS, 2 * DW + 1)
    return jnp.pad(coefs, ((0, 0), (0, 1), (0, Q_BLOCK - 2 * DW - 1)))


def fill_taps(coef_ref, window_refs, band_ref, taps_ref):
    for k in range(K):
        for place in range(N_LAT_TAPS):
            index = k * N_LAT_TAPS + place
            row = jnp.broadcast_to(coef_ref[0, index : index + 1, :], (P_BLOCK, Q_BLOCK))
            band = pltpu.roll(row, 0, 1, stride=1, stride_axis=0)
            band_ref[
                k * P_BLOCK : (k + 1) * P_BLOCK, place * Q_BLOCK : (place + 1) * Q_BLOCK
            ] = band.astype(jnp.bfloat16)
    col_count, wide = taps_ref.shape
    chan_count = wide // K
    for start in range(0, col_count, P_BLOCK):
        window = jnp.concatenate([ref[0, start : start + Q_BLOCK, :] for ref in window_refs], axis=0)
        summed = jnp.dot(band_ref[...], window, preferred_element_type=jnp.float32)
        for k in range(K):
            taps_ref[start : start + P_BLOCK, k * chan_count : (k + 1) * chan_count] = summed[
                k * P_BLOCK : (k + 1) * P_BLOCK
            ].astype(jnp.bfloat16)


def conv_kernel(coef_ref, w0, w1, w2, w3, w4, weight_ref, conv_ref, band_ref, taps_ref):
    fill_taps(coef_ref, (w0, w1, w2, w3, w4), band_ref, taps_ref)
    conv_ref[0] = jnp.dot(
        taps_ref[...], weight_ref[...], preferred_element_type=jnp.float32
    ).astype(jnp.bfloat16)


def back_kernel(
    coef_ref, w0, w1, w2, w3, w4, weight_ref, source_ref, input_ref, weight_grad_ref, band_ref, taps_ref
):
    fill_taps(coef_ref, (w0, w1, w2, w3, w4), band_ref, taps_ref)
    input_ref[0] = jnp.dot(
        taps_ref[...], weight_ref[...], preferred_element_type=jnp.float32
    ).astype(jnp.bfloat16)

    @pl.when(pl.program_id(0) == 0)
    def _():
        weight_grad_ref[...] = jnp.zeros_like(weight_grad_ref)

    weight_grad_ref[...] += lax.dot_general(
        source_ref[0], taps_ref[...], (((0,), (0,)), ((), ())), preferred_element_type=jnp.float32
    )


def tap_call(kernel, padded, coefs, flat_weight, col_count, source=None):
    row_count = coefs.shape[0]
    wide_count, chan_count = padded.shape[1:]

    def window_spec(place):
        return pl.BlockSpec((1, wide_count, chan_count), lambda t: (t + place, 0, 0))

    row_spec = pl.BlockSpec((1, col_count, chan_count), lambda t: (t, 0, 0))
    in_specs = [pl.BlockSpec((1,) + coefs.shape[1:], lambda t: (t, 0, 0))]
    in_specs += [window_spec(place) for place in range(N_LAT_TAPS)]
    in_specs += [pl.BlockSpec(flat_weight.shape, lambda t: (0, 0))]
    operands = [coefs] + [padded] * N_LAT_TAPS + [flat_weight]
    row_shape = jax.ShapeDtypeStruct((row_count, col_count, chan_count), jnp.bfloat16)
    positions = row_count * col_count
    flops = 2 * positions * chan_count * K * (N_LAT_TAPS * Q_BLOCK + chan_count)
    if source is None:
        out_specs, out_shape = row_spec, row_shape
    else:
        in_specs.append(row_spec)
        operands.append(source)
        grad_shape = (chan_count, K * chan_count)
        out_specs = (row_spec, pl.BlockSpec(grad_shape, lambda t: (0, 0)))
        out_shape = (row_shape, jax.ShapeDtypeStruct(grad_shape, jnp.float32))
        flops += 2 * positions * chan_count * K * chan_count
    return pl.pallas_call(
        kernel,
        grid=(row_count,),
        in_specs=in_specs,
        out_specs=out_specs,
        out_shape=out_shape,
        scratch_shapes=[
            pltpu.VMEM((K * P_BLOCK, N_LAT_TAPS * Q_BLOCK), jnp.bfloat16),
            pltpu.VMEM((col_count, K * chan_count), jnp.bfloat16),
        ],
        compiler_params=pltpu.CompilerParams(vmem_limit_bytes=48 * 1024 * 1024),
        cost_estimate=pl.CostEstimate(
            flops=flops, bytes_accessed=2 * 8 * positions * chan_count, transcendentals=0
        ),
    )(*operands)


def padded_field(field):
    lon_padded = extended(field, (("lon", 1),), DW, True)
    lon_padded = jnp.pad(lon_padded, ((0, 0), (0, Q_BLOCK - P_BLOCK - 2 * DW), (0, 0)))
    return extended(lon_padded, (("lat", 0),), H, False)


def to_lines(field):
    count = lax.axis_size("lon")
    parts = field.reshape((count, field.shape[0] // count) + field.shape[1:])
    return lax.all_to_all(parts, "lon", split_axis=0, concat_axis=0, tiled=True)


def to_grid(parts):
    moved = lax.all_to_all(parts, "lon", split_axis=0, concat_axis=0, tiled=True)
    return moved.reshape((-1,) + parts.shape[2:])


def to_spec(field):
    count = lax.axis_size("lat") * lax.axis_size("lon")
    rows, cols, chans = field.shape
    parts = field.reshape(rows, count, cols // count, chans).transpose(1, 0, 2, 3)
    moved = lax.all_to_all(parts, ("lat", "lon"), split_axis=0, concat_axis=0, tiled=True)
    return moved.reshape(count * rows, cols // count, chans)


def to_line_rows(field):
    count = lax.axis_size("lat") * lax.axis_size("lon")
    rows, cols, chans = field.shape
    parts = field.reshape(count, rows // count, cols, chans)
    moved = lax.all_to_all(parts, ("lat", "lon"), split_axis=0, concat_axis=0, tiled=True)
    return moved.transpose(1, 0, 2, 3).reshape(rows // count, count * cols, chans)


def legendre_in(spectral, table_rows):
    lat_total, col_total, chan_total = spectral.shape
    halves = spectral.reshape(lat_total, col_total // 2, 2, chan_total)
    return jnp.einsum("olt,toqc->olqc", table_rows, halves, preferred_element_type=jnp.float32)


def legendre_out(coefficients, table_rows):
    synthesis = jnp.einsum(
        "olt,olqc->toqc", table_rows, coefficients, preferred_element_type=jnp.float32
    )
    lat_total, order_count, two_parts, chan_total = synthesis.shape
    return synthesis.reshape(lat_total, order_count * two_parts, chan_total)


def body(
    source_field,
    cotangent,
    weight,
    spectral_gain,
    legendre,
    support_lat,
    support_lon,
    support_val,
    order_map,
):
    row_count, col_count, chan_count = source_field.shape
    lon_devices = lax.axis_size("lon")
    lat_total = row_count * lax.axis_size("lat")
    band_index = lax.axis_index("lat")
    block_index = lax.axis_index("lon")
    tap_weights = tap_table(support_lat, support_lon, support_val)
    tap_pad = jnp.pad(tap_weights, ((H, H), (0, 0), (0, 0), (0, 0)))
    tap_rows = lax.dynamic_slice_in_dim(tap_pad, band_index * row_count, row_count + 2 * H, 0)
    dft_matrix = dft_table(order_map)
    dft_parts = dft_matrix.reshape(lon_devices, col_count, dft_matrix.shape[1])
    flat_weight = weight.reshape(K * chan_count, chan_count)
    flat_weight_back = weight.transpose(0, 2, 1).reshape(K * chan_count, chan_count)
    all_rows = jnp.arange(lat_total, dtype=jnp.int32).astype(jnp.float32)
    quad_all = jnp.sin(math.pi * (all_rows + 0.5) / lat_total)
    line_rows = row_count // lon_devices
    line_quad = lax.dynamic_slice_in_dim(
        quad_all, band_index * row_count + block_index * line_rows, line_rows, 0
    )
    cot_line_spec = jnp.einsum(
        "nrpc,npj->rjc", to_lines(cotangent), dft_parts, preferred_element_type=jnp.float32
    )
    cot_spectral = to_spec(cot_line_spec.astype(jnp.bfloat16))
    conv_out = tap_call(
        conv_kernel,
        padded_field(source_field),
        tap_coefficients(tap_rows, row_count, False),
        flat_weight,
        col_count,
    )
    conv_wide = conv_out.astype(jnp.float32)
    hidden = gelu_value(conv_wide).astype(jnp.bfloat16)
    line_spec = jnp.einsum(
        "nrpc,npj->rjc", to_lines(hidden), dft_parts, preferred_element_type=jnp.float32
    )
    spectral = to_spec((line_spec * line_quad[:, None, None]).astype(jnp.bfloat16))
    cot_coefficients = legendre_in(cot_spectral, legendre)
    cot_filtered = (spectral_gain[None, :, None, :] * cot_coefficients).astype(jnp.bfloat16)
    cot_synth = legendre_out(cot_filtered, legendre)
    cot_synth = (cot_synth * quad_all[:, None, None]).astype(jnp.bfloat16)
    cot_synth_lines = to_line_rows(cot_synth)
    coefficients = legendre_in(spectral, legendre)
    gain_part = jnp.sum(coefficients * cot_coefficients, axis=(0, 2))
    filtered = (spectral_gain[None, :, None, :] * coefficients).astype(jnp.bfloat16)
    synth_lines = to_line_rows(legendre_out(filtered, legendre).astype(jnp.bfloat16))
    cot_hidden = jnp.einsum(
        "rjc,npj->nrpc", cot_synth_lines, dft_parts, preferred_element_type=jnp.float32
    ).astype(jnp.bfloat16)
    cot_hidden_grid = to_grid(cot_hidden)
    cot_conv = (
        cotangent.astype(jnp.float32) + cot_hidden_grid.astype(jnp.float32) * gelu_slope(conv_wide)
    ).astype(jnp.bfloat16)
    grad_input, weight_part = tap_call(
        back_kernel,
        padded_field(cot_conv),
        tap_coefficients(tap_rows, row_count, True),
        flat_weight_back,
        col_count,
        source_field,
    )
    branch = jnp.einsum(
        "rjc,npj->nrpc", synth_lines, dft_parts, preferred_element_type=jnp.float32
    ).astype(jnp.bfloat16)
    result = (conv_wide + to_grid(branch).astype(jnp.float32)).astype(jnp.bfloat16)
    weight_total = lax.psum(weight_part, ("lat", "lon")).reshape(chan_count, K, chan_count)
    gain_total = lax.psum(gain_part, ("lat", "lon"))
    grad_weight = weight_total.transpose(1, 0, 2) / math.sqrt(1.0 * lat_total * NLON)
    grad_gain = gain_total / math.sqrt(2.0 * M)
    return (result, grad_input, grad_weight, grad_gain)


def solution(mesh):
    return jax.shard_map(
        body,
        mesh=mesh,
        in_specs=(
            P("lat", "lon", None),
            P("lat", "lon", None),
            P(),
            P(),
            P(("lat", "lon"), None, None),
            P(),
            P(),
            P(),
            P(),
        ),
        out_specs=(P("lat", "lon", None), P("lat", "lon", None), P(), P()),
        check_vma=False,
    )
```

time: 2660 us -> 1370 us (0.52)
  matrix products: 1260 us -> 127 us
  local copies, waits for them, and re-layouts: 448 us -> 187 us
  Pallas kernels: 0 us -> 99 us
  other arithmetic: 141 us -> 61 us
  blocking collectives: 7.61 us -> 81.5 us
    dot_general x7 -> x4, matrix products: 1130 us -> 71 us  [the longest x1 18.3 us: body(): jnp.einsum('nrpc,npj->rjc', to_lines(hidden), dft_parts, preferred_elemen...]
    convert_element_type x15 -> x2, local copies, waits for them, and re-layouts: 219 us -> 47.9 us  [body(): legendre_out(filtered, legendre).astype(jnp.bfloat16)]
    all_to_all x12 -> x0, local copies, waits for them, and re-layouts: 137 us -> none  [the longest x4 55.7 us: to_lines(): lax.all_to_all(field, 'lon', split_axis=2, concat_axis=1, tiled=True)]
    psum x2 -> x1, waiting for transfers between devices: 0.01 us -> 135 us  [body(): lax.psum(weight_part, ('lat', 'lon')).reshape(chan_count, K, chan_count)]
    all_to_all x8 -> x7, waiting for transfers between devices: 688 us -> 574 us  [the longest x2 199 us: to_spec(): lax.all_to_all(parts, ('lat', 'lon'), split_axis=0, concat_axis=0, tiled=...]
    pallas_call x0 -> x2, Pallas kernels: none -> 99 us  [tap_call(): pl.pallas_call(kernel, grid=(row_count,), in_specs=in_specs, out_specs=ou...]
    all_to_all x0 -> x1, blocking collectives: none -> 81.5 us  [to_grid(): lax.all_to_all(parts, 'lon', split_axis=0, concat_axis=0, tiled=True)]
    unnamed x4 -> x0, matrix products: 79.3 us -> none
  transfers between devices with their start and end apart: 19 -> 16, of which waited for: 8 -> 12; matrix products, arithmetic and copies ran while one was open for 63% -> 23% of each run, Pallas kernels for 0% -> 0%
where the time goes in v1:
time: 1370 us; the launch traced here: 1350 us
  waiting for transfers between devices  716 us (52%)
  local copies, waits for them, and re-layouts  187 us (14%)
  matrix products  127 us (9%)
  Pallas kernels  99 us (7%)
  blocking collectives  81.5 us (6%)
  starting transfers between devices  66 us (5%)
  other arithmetic  61 us (4%)
  between operations  14.7 us (1%)
    all_to_all x2, waiting for transfers between devices, to_spec(): lax.all_to_all(parts, ('lat', 'lon'), split_axis=0, concat_axis=0, tiled=...  199 us
    all_to_all x2, waiting for transfers between devices, to_line_rows(): lax.all_to_all(parts, ('lat', 'lon'), split_axis=0, concat_axis=0, tiled=...  189 us
    psum x1, waiting for transfers between devices, body(): lax.psum(weight_part, ('lat', 'lon')).reshape(chan_count, K, chan_count)  135 us
    all_to_all x2, waiting for transfers between devices, to_lines(): return lax.all_to_all(parts, 'lon', split_axis=0, concat_axis=0, tiled=True)  129 us
    pallas_call x2, Pallas kernels, tap_call(): pl.pallas_call(kernel, grid=(row_count,), in_specs=in_specs, out_specs=ou...  99 us
    all_to_all x1, blocking collectives, to_grid(): lax.all_to_all(parts, 'lon', split_axis=0, concat_axis=0, tiled=True)  81.5 us
    all_to_all x1, waiting for transfers between devices, to_grid(): lax.all_to_all(parts, 'lon', split_axis=0, concat_axis=0, tiled=True)  56.5 us
    convert_element_type x2, local copies, waits for them, and re-layouts, body(): legendre_out(filtered, legendre).astype(jnp.bfloat16)  47.9 us
  transfers between devices with their start and end apart: 16, of which 12 were waited for; matrix products, arithmetic and copies ran while one was open for 23% of the time, Pallas kernels for 0%

profile of v1, /device:TPU:9, one launch (start us, length us, event | category | flops | bytes accessed | tf_op | source)
XLA Modules:
  0.0 1352.2 jit_solution(7807345597457461757)
XLA Ops:
  44.7 7.7 pad_maximum_fusion.w0.w1.w2.w3.w4
  52.4 40.9 %shard_map.120 = bf16[24,384,384]{2,1,0:T(8,128)(2,1)} custom-call(f32[24,16,128]{2,1,0:T(8,128)S(1)} %pad.19.coef_ref, bf16[28,416,384]{2,1,0:T(8,128)(2,1)} %pad_maximum_fusion.w0.w1.w2.w3.w4, bf16[28,416,384]{2,1,0:T(8,128)(2,1)} %pad_maximum_fusion.w0.w1.w2.w3.w4, bf16[28,416,384]{2,1,0:T(8,128)(2,1)} %pad_maximum_fusion.w0.w1.w2.w3.w4, ...), custom_call_target="tpu_custom_call" | custom-call | flops 21743271936 | bytes 56623104 | tf_op jit(solution)/shard_map/pallas_call | solution.py:153
  93.3 7.8 fusion.7
  109.7 74.0 %all-to-all-done = bf16[2,12,384,384]{3,2,1,0:T(8,128)(2,1)} async-done(((bf16[2,12,384,384]{3,2,1,0:T(8,128)(2,1)}), bf16[2,12,384,384]{3,2,1,0:T(8,128)(2,1)}, u32[]{:S(2)}, u32[]{:S(2)}) %all-to-all-start) | async-done | bytes 7077920 | tf_op jit(solution)/shard_map/all_to_all | solution.py:179
  190.6 18.3 %fusion.17 = bf16[768,12,384]{2,0,1:T(8,128)(2,1)S(1)} fusion(bf16[2,12,384,384]{3,2,1,0:T(8,128)(2,1)} %all-to-all-done, f32[12]{0:T(128)S(1)} %dynamic_slice.7, s32[768]{0:T(1024)S(1)} %mul.135, s32[2,384]{1,0:T(2,128)S(1)} %multiply_add_fusion, pred[768]{0:T(1024)(128)(4,1)S(1)} %fusion.75), kind=kOutput, calls=%fused_computation.26 | convolution fusion | flops 5450563584 | bytes 14162736 | tf_op jit(solution)/shard_map/nrpc,npj->rjc/dot_general | solution.py:259
  212.5 55.2 %all-to-all-done.4 = bf16[2,12,384,384]{3,2,1,0:T(8,128)(2,1)} async-done(((bf16[2,12,384,384]{3,2,1,0:T(8,128)(2,1)}), bf16[2,12,384,384]{3,2,1,0:T(8,128)(2,1)}, u32[]{:S(2)}, u32[]{:S(2)}) %all-to-all-start.4) | async-done | bytes 7077920 | tf_op jit(solution)/shard_map/all_to_all | solution.py:179
  272.1 18.2 %bitcast_convert_fusion = bf16[768,12,384]{2,0,1:T(8,128)(2,1)S(1)} fusion(bf16[2,12,384,384]{3,2,1,0:T(8,128)(2,1)} %all-to-all-done.4, s32[768]{0:T(1024)S(1)} %mul.135, s32[2,384]{1,0:T(2,128)S(1)} %multiply_add_fusion, pred[768]{0:T(1024)(128)(4,1)S(1)} %fusion.75), kind=kOutput, calls=%fused_computation.24 | convolution fusion | flops 5447024640 | bytes 14162688 | tf_op jit(solution)/shard_map/nrpc,npj->rjc/dot_general | solution.py:246
  293.9 132.7 %all-to-all-done.1 = bf16[32,12,24,384]{3,2,1,0:T(8,128)(2,1)} async-done(((bf16[32,12,24,384]{3,2,1,0:T(8,128)(2,1)}), bf16[32,12,24,384]{3,2,1,0:T(8,128)(2,1)}, u32[]{:S(2)}, u32[]{:S(2)}) %all-to-all-start.1) | async-done | bytes 7077920 | tf_op jit(solution)/shard_map/all_to_all | solution.py:191
  426.6 7.9 all-to-all-start.5
  436.7 14.7 %reshape_reshape.6 = bf16[384,12,2,384]{3,2,1,0:T(2,128)(2,1)} reshape(bf16[32,12,24,384]{3,2,1,0:T(8,128)(2,1)} %all-to-all-done.1) | data formatting | bytes 14155776 | tf_op jit(solution)/shard_map/reshape;reshape | solution.py:205
  451.4 10.2 fusion.30
  461.6 13.1 convert_bitcast_fusion.2
  474.6 32.7 %copy.102 = bf16[384,12,2,384]{3,2,1,0:T(2,128)(2,1)} copy(bf16[384,12,2,384]{3,0,2,1:T(8,128)(2,1)} %convert_bitcast_fusion.2) | data formatting | bytes 14155776 | tf_op jit(solution)/shard_map/convert_element_type | solution.py:271
  507.3 15.2 %convert_element_type.118 = bf16[32,12,24,384]{3,2,1,0:T(8,128)(2,1)} reshape(bf16[384,12,2,384]{3,2,1,0:T(2,128)(2,1)} %copy.102) | data formatting | bytes 14155776 | tf_op jit(solution)/shard_map/convert_element_type | solution.py:271
  522.5 66.6 %all-to-all-done.5 = bf16[32,12,24,384]{3,2,1,0:T(8,128)(2,1)} async-done(((bf16[32,12,24,384]{3,2,1,0:T(8,128)(2,1)}), bf16[32,12,24,384]{3,2,1,0:T(8,128)(2,1)}, u32[]{:S(2)}, u32[]{:S(2)}) %all-to-all-start.5) | async-done | bytes 7077920 | tf_op jit(solution)/shard_map/all_to_all | solution.py:191
  596.9 14.7 %reshape_reshape.7 = bf16[384,12,2,384]{3,2,1,0:T(2,128)(2,1)} reshape(bf16[32,12,24,384]{3,2,1,0:T(8,128)(2,1)} %all-to-all-done.5) | data formatting | bytes 14155776 | tf_op jit(solution)/shard_map/reshape;reshape | solution.py:205
  611.6 13.8 %fusion.19 = (f32[384,384]{0,1:T(8,128)}, f32[12,2,384,384]{3,2,1,0:T(8,128)}) fusion(f32[12,2,384,384]{3,2,1,0:T(8,128)} %fusion.30, bf16[12,384,384]{2,1,0:T(8,128)(2,1)S(1)} %copy-done, bf16[384,12,2,384]{3,2,1,0:T(2,128)(2,1)} %reshape_reshape.7), kind=kOutput, calls=%fused_computation.30 | convolution fusion | flops 2724839424 | bytes 39518208 | tf_op jit(solution)/shard_map/olt,toqc->olqc/dot_general | solution.py:206
  625.4 14.7 %convolution_bitcast_fusion = f32[384,12,2,384]{3,0,2,1:T(8,128)} fusion(f32[12,2,384,384]{3,2,1,0:T(8,128)} %get-tuple-element.38, f32[384,384]{0,1:T(8,128)S(1)} %copy-done.7, bf16[12,384,384]{2,1,0:T(8,128)(2,1)S(1)} %copy-done), kind=kOutput, calls=%fused_computation.36 | convolution fusion | flops 2724986880 | bytes 32440320 | tf_op jit(solution)/shard_map/olt,olqc->toqc/dot_general | solution.py:210
  640.0 28.9 %copy.112 = f32[384,12,2,384]{3,2,1,0:T(2,128)} copy(f32[384,12,2,384]{3,0,2,1:T(8,128)} %convolution_bitcast_fusion) | data formatting | bytes 28311552 | tf_op jit(solution)/shard_map/olt,olqc->toqc/transpose | solution.py:210
  668.9 17.4 %reshape.135 = f32[32,12,24,384]{3,2,1,0:T(8,128)} reshape(f32[384,12,2,384]{3,2,1,0:T(2,128)} %copy.112) | data formatting | bytes 28311552 | tf_op jit(solution)/shard_map/reshape | solution.py:214
  686.4 8.9 multiply_convert_fusion
  695.3 56.1 %all-to-all-done.2 = bf16[32,12,24,384]{3,2,1,0:T(8,128)(2,1)} async-done(((bf16[32,12,24,384]{3,2,1,0:T(8,128)(2,1)}), bf16[32,12,24,384]{3,2,1,0:T(8,128)(2,1)}, u32[]{:S(2)}, u32[]{:S(2)}) %all-to-all-start.2) | async-done | bytes 7077920 | tf_op jit(solution)/shard_map/all_to_all | solution.py:199
  751.4 7.7 all-to-all-start.6
  763.4 17.3 %convert_bitcast_fusion.1 = bf16[2,12,384,384]{3,2,1,0:T(8,128)(2,1)} fusion(bf16[12,768,384,1]{2,1,0,3:T(8,128)(2,1)S(1)} %bitcast.127, s32[768]{0:T(1024)S(1)} %copy-done.12, s32[2,384]{1,0:T(2,128)S(1)} %copy-done.14, pred[768]{0:T(1024)(128)(4,1)S(1)} %copy-done.17), kind=kOutput, calls=%fused_computation.49 | convolution fusion | flops 5447024640 | bytes 14162688 | tf_op jit(solution)/shard_map/rjc,npj->nrpc/dot_general | solution.py:287
  780.6 133.1 %all-to-all-done.6 = bf16[32,12,24,384]{3,2,1,0:T(8,128)(2,1)} async-done(((bf16[32,12,24,384]{3,2,1,0:T(8,128)(2,1)}), bf16[32,12,24,384]{3,2,1,0:T(8,128)(2,1)}, u32[]{:S(2)}, u32[]{:S(2)}) %all-to-all-start.6) | async-done | bytes 7077920 | tf_op jit(solution)/shard_map/all_to_all | solution.py:199
  924.6 17.2 %convert_bitcast_fusion = bf16[2,12,384,384]{3,2,1,0:T(8,128)(2,1)} fusion(bf16[12,768,384,1]{2,1,0,3:T(8,128)(2,1)S(1)} %bitcast.124, s32[768]{0:T(1024)S(1)} %copy-done.12, s32[2,384]{1,0:T(2,128)S(1)} %copy-done.14, pred[768]{0:T(1024)(128)(4,1)S(1)} %copy-done.17), kind=kOutput, calls=%fused_computation.48 | convolution fusion | flops 5447024640 | bytes 14162688 | tf_op jit(solution)/shard_map/rjc,npj->nrpc/dot_general | solution.py:272
  941.8 56.5 %all-to-all-done.3 = bf16[2,12,384,384]{3,2,1,0:T(8,128)(2,1)} async-done(((bf16[2,12,384,384]{3,2,1,0:T(8,128)(2,1)}), bf16[2,12,384,384]{3,2,1,0:T(8,128)(2,1)}, u32[]{:S(2)}, u32[]{:S(2)}) %all-to-all-start.3) | async-done | bytes 7077920 | tf_op jit(solution)/shard_map/all_to_all | solution.py:183
  998.3 81.5 %all_to_all.40 = bf16[2,12,384,384]{3,2,1,0:T(8,128)(2,1)S(1)} all-to-all(bf16[2,12,384,384]{3,2,1,0:T(8,128)(2,1)} %convert_bitcast_fusion), channel_id=1, replica_groups=mesh['lat'=16,'lon'=2] {'lon'}, dimensions={0} | all-to-all | bytes 14155776 | tf_op jit(solution)/shard_map/all_to_all | solution.py:183
  1079.8 14.2 %fusion.15 = (bf16[24,384,384]{2,1,0:T(8,128)(2,1)S(1)}, bf16[24,384,384]{2,1,0:T(8,128)(2,1)}) fusion(bf16[24,384,384]{2,1,0:T(8,128)(2,1)} %shard_map.120, bf16[24,384,384]{2,1,0:T(8,128)(2,1)} %param.10, bf16[2,12,384,384]{3,2,1,0:T(8,128)(2,1)S(1)} %all_to_all.40, bf16[2,12,384,384]{3,2,1,0:T(8,128)(2,1)} %all-to-all-done.3), kind=kLoop, calls=%fused_computation.22 | loop fusion | flops 60162048 | bytes 42467328 | tf_op jit(solution)/shard_map/convert_element_type | solution.py:278
  1130.6 7.8 pad_maximum_fusion.1.w0.w1.w2.w3.w4
  1138.5 58.1 %shard_map.121 = (bf16[24,384,384]{2,1,0:T(8,128)(2,1)}, f32[384,1152]{1,0:T(8,128)S(1)}) custom-call(f32[24,16,128]{2,1,0:T(8,128)S(1)} %pad.21.coef_ref, bf16[28,416,384]{2,1,0:T(8,128)(2,1)} %pad_maximum_fusion.1.w0.w1.w2.w3.w4, bf16[28,416,384]{2,1,0:T(8,128)(2,1)} %pad_maximum_fusion.1.w0.w1.w2.w3.w4, ...), custom_call_target="tpu_custom_call" | custom-call | flops 29896998912 | bytes 56623104 | tf_op jit(solution)/shard_map/pallas_call | solution.py:153
  1197.8 134.8 %all-reduce.8.cloned.1.call-done = (f32[384,1152]{1,0:T(8,128)}, f32[384,384]{0,1:T(8,128)}) async-done(((f32[384,1152]{1,0:T(8,128)}, f32[384,384]{0,1:T(8,128)}), (f32[384,1152]{1,0:T(8,128)}, f32[384,384]{0,1:T(8,128)})) %all-reduce.8.cloned.1.call-update) | async-done | bytes 2359312 | tf_op jit(solution)/shard_map/psum | solution.py:291
  (102 shorter events, 139.7 us)
Async XLA Ops:
  7.2 444.2 %copy-start = (bf16[12,384,384]{2,1,0:T(8,128)(2,1)S(1)}, bf16[12,384,384]{2,1,0:T(8,128)(2,1)}, u32[]{:S(2)}) copy-start(bf16[12,384,384]{2,1,0:T(8,128)(2,1)} %param.13) | copy-start | bytes 10616836
  9.0 8.9 collective-permute-start
  10.2 7.7 collective-permute-start.1
  17.9 12.7 copy-start.8
  17.9 12.7 copy-start.9
  17.9 12.7 copy-start.10
  23.0 7.5 copy-start.6
  24.3 18.8 %collective-permute-start.2 = (bf16[2,416,384]{2,1,0:T(8,128)(2,1)}, bf16[2,416,384]{2,1,0:T(8,128)(2,1)}, u32[]{:S(2)}, u32[]{:S(2)}) collective-permute-start(bf16[2,416,384]{2,1,0:T(8,128)(2,1)} %get-tuple-element.24), channel_id=1, source_target_pairs={{0,2},{2,4},{4,6},{6,8},{8,10},{10,12},{12,14},{14,16},{16,18},{18... | collective-permute-start | bytes 1916936 | tf_op jit(solution)/shard_map/ppermute | solution.py:28
  28.6 16.1 %collective-permute-start.3 = (bf16[2,416,384]{2,1,0:T(8,128)(2,1)}, bf16[2,416,384]{2,1,0:T(8,128)(2,1)}, u32[]{:S(2)}, u32[]{:S(2)}) collective-permute-start(bf16[2,416,384]{2,1,0:T(8,128)(2,1)} %get-tuple-element.25), channel_id=1, source_target_pairs={{2,0},{4,2},{6,4},{8,6},{10,8},{12,10},{14,12},{16,14},{18,16},{20... | collective-permute-start | bytes 1916936 | tf_op jit(solution)/shard_map/ppermute | solution.py:31
  40.1 12.3 copy-start.2
  101.0 6.7 copy-start.15
  101.0 82.7 %all-to-all-start = ((bf16[2,12,384,384]{3,2,1,0:T(8,128)(2,1)}), bf16[2,12,384,384]{3,2,1,0:T(8,128)(2,1)}, u32[]{:S(2)}, u32[]{:S(2)}) async-start(bf16[2,12,384,384]{3,2,1,0:T(8,128)(2,1)} %bitcast.120), calls=%async_computation | async-start | bytes 14155776 | tf_op jit(solution)/shard_map/all_to_all | solution.py:179
  109.6 162.5 %copy-start.11 = (s32[768]{0:T(1024)}, s32[768]{0:T(1024)S(1)}, u32[]{:S(2)}) copy-start(s32[768]{0:T(1024)S(1)} %mul.135) | copy-start | bytes 9220
  109.7 162.4 %copy-start.16 = (pred[768]{0:T(1024)(128)(4,1)}, pred[768]{0:T(1024)(128)(4,1)S(1)}, u32[]{:S(2)}) copy-start(pred[768]{0:T(1024)(128)(4,1)S(1)} %fusion.75) | copy-start | bytes 2308
  109.7 162.4 %copy-start.13 = (s32[2,384]{1,0:T(2,128)}, s32[2,384]{1,0:T(2,128)S(1)}, u32[]{:S(2)}) copy-start(s32[2,384]{1,0:T(2,128)S(1)} %multiply_add_fusion) | copy-start | bytes 9220
  183.7 84.0 %all-to-all-start.4 = ((bf16[2,12,384,384]{3,2,1,0:T(8,128)(2,1)}), bf16[2,12,384,384]{3,2,1,0:T(8,128)(2,1)}, u32[]{:S(2)}, u32[]{:S(2)}) async-start(bf16[2,12,384,384]{3,2,1,0:T(8,128)(2,1)} %bitcast.123), calls=%async_computation.4 | async-start | bytes 14155776 | tf_op jit(solution)/shard_map/all_to_all | solution.py:179
  267.7 158.9 %all-to-all-start.1 = ((bf16[32,12,24,384]{3,2,1,0:T(8,128)(2,1)}), bf16[32,12,24,384]{3,2,1,0:T(8,128)(2,1)}, u32[]{:S(2)}, u32[]{:S(2)}) async-start(bf16[32,12,24,384]{3,2,1,0:T(8,128)(2,1)} %bitcast.122), calls=%async_computation.1 | async-start | bytes 14155776 | tf_op jit(solution)/shard_map/all_to_all | solution.py:191
  426.6 162.5 %all-to-all-start.5 = ((bf16[32,12,24,384]{3,2,1,0:T(8,128)(2,1)}), bf16[32,12,24,384]{3,2,1,0:T(8,128)(2,1)}, u32[]{:S(2)}, u32[]{:S(2)}) async-start(bf16[32,12,24,384]{3,2,1,0:T(8,128)(2,1)} %bitcast.121), calls=%async_computation.5 | async-start | bytes 14155776 | tf_op jit(solution)/shard_map/all_to_all | solution.py:191
  589.1 162.3 %all-to-all-start.2 = ((bf16[32,12,24,384]{3,2,1,0:T(8,128)(2,1)}), bf16[32,12,24,384]{3,2,1,0:T(8,128)(2,1)}, u32[]{:S(2)}, u32[]{:S(2)}) async-start(bf16[32,12,24,384]{3,2,1,0:T(8,128)(2,1)} %convert_element_type.118), calls=%async_computation.2 | async-start | bytes 14155776 | tf_op jit(solution)/shard_map/all_to_all | solution.py:199
  611.6 13.8 %copy-start.7 = (f32[384,384]{0,1:T(8,128)S(1)}, f32[384,384]{0,1:T(8,128)}, u32[]{:S(2)}) copy-start(f32[384,384]{0,1:T(8,128)} %copy.95) | copy-start | bytes 1769476
  751.4 162.3 %all-to-all-start.6 = ((bf16[32,12,24,384]{3,2,1,0:T(8,128)(2,1)}), bf16[32,12,24,384]{3,2,1,0:T(8,128)(2,1)}, u32[]{:S(2)}, u32[]{:S(2)}) async-start(bf16[32,12,24,384]{3,2,1,0:T(8,128)(2,1)} %multiply_convert_fusion), calls=%async_computation.6 | async-start | bytes 14155776 | tf_op jit(solution)/shard_map/all_to_all | solution.py:199
  759.1 4.2 copy-start.12
  759.2 4.2 copy-start.14
  759.2 4.2 copy-start.17
  913.7 84.6 %all-to-all-start.3 = ((bf16[2,12,384,384]{3,2,1,0:T(8,128)(2,1)}), bf16[2,12,384,384]{3,2,1,0:T(8,128)(2,1)}, u32[]{:S(2)}, u32[]{:S(2)}) async-start(bf16[2,12,384,384]{3,2,1,0:T(8,128)(2,1)} %convert_bitcast_fusion.1), calls=%async_computation.3 | async-start | bytes 14155776 | tf_op jit(solution)/shard_map/all_to_all | solution.py:183
  920.4 412.2 %all-reduce.8.cloned.1.call-start = ((), (), s32[]{:S(2)}) async-start(), calls=%async_computation.8 | async-start | bytes 4718592 | tf_op jit(solution)/shard_map/psum | solution.py:291
  1094.0 3.3 collective-permute-start.4
  1094.4 3.7 collective-permute-start.5
  1100.4 3.0 copy-start.5
  1104.6 26.0 %collective-permute-start.6 = (bf16[2,416,384]{2,1,0:T(8,128)(2,1)}, bf16[2,416,384]{2,1,0:T(8,128)(2,1)}, u32[]{:S(2)}, u32[]{:S(2)}) collective-permute-start(bf16[2,416,384]{2,1,0:T(8,128)(2,1)} %get-tuple-element.22), channel_id=1, source_target_pairs={{0,2},{2,4},{4,6},{6,8},{8,10},{10,12},{12,14},{14,16},{16,18},{18... | collective-permute-start | bytes 1916936 | tf_op jit(solution)/shard_map/ppermute | solution.py:28
  1111.5 19.2 %collective-permute-start.7 = (bf16[2,416,384]{2,1,0:T(8,128)(2,1)}, bf16[2,416,384]{2,1,0:T(8,128)(2,1)}, u32[]{:S(2)}, u32[]{:S(2)}) collective-permute-start(bf16[2,416,384]{2,1,0:T(8,128)(2,1)} %get-tuple-element.23), channel_id=1, source_target_pairs={{2,0},{4,2},{6,4},{8,6},{10,8},{12,10},{14,12},{16,14},{18,16},{20... | collective-permute-start | bytes 1916936 | tf_op jit(solution)/shard_map/ppermute | solution.py:31
  1130.6 7.8 copy-start.3
  (2 other events, 3.4 us)
Sparse Core Ops, SparseCore 0:
  1197.9 134.6 all-reduce.7
